TPU v7x, 512 devices: a whole 4x4x16 slice. The times are simulated.
512 devices in a mesh: stn: 64 (over y_hi, z, core), blk: 8 (over y_lo, x).
Axes of the slice: x: 4, y: 4 (y_hi: 2, y_lo: 2; y = y_hi * 2 + y_lo), z: 16, core: 2. Of those that a mesh axis runs over, the one named last changes fastest.
Arguments:
- samples: int32 [2, 512, 262144], P(None, 'stn', 'blk'), may hold values from -128 to 127, as said below
- fir_taps: float32 [8, 1024], replicated, may hold values from -2 to 2
- station_order: int32 [512], replicated, may hold values from 0 to 511, each once
Outputs:
- coherence: bfloat16 [2, 1024, 512, 512], P(None, 'stn', 'blk')
Inputs may be any that keep to these rules, and one draw needn't show every extreme that they name: `samples`: quantized voltages, real parts in row 0 and imaginary parts in row 1 of the leading dimension. `station_order`: each station number appears exactly once.
All inputs are finite; a program needn't handle non-finite values.
Results may differ from a plain program's by a relative error of at most 0.0033.
Values may be sent and summed in bfloat16 or wider, within the bound.
A program may use at most 64 MiB of HBM per device.

v0:
```python
import math

import jax
import jax.numpy as jnp
from jax import lax
from jax.sharding import PartitionSpec as P

epsilon = 1e-06


def passed_along(value, axis, steps):
    count = lax.axis_size(axis)
    initial, last = (max(0, -steps), min(count, count - steps))
    return lax.ppermute(value, axis, [(source, source + steps) for source in range(initial, last)])


def dft_tables(channels):
    channel_index = jnp.arange(channels, dtype=jnp.int32)
    phase_index = channel_index[:, None] * channel_index[None, :] % channels
    angle_table = phase_index.astype(jnp.float32) * (2.0 * math.pi / channels)
    return (jnp.cos(angle_table).astype(jnp.bfloat16), jnp.sin(angle_table).astype(jnp.bfloat16))


def correlate(row_block, column_block):
    swapped = jnp.stack([row_block[1], -row_block[0]])
    left_side = jnp.stack([row_block, swapped])
    return jnp.einsum(
        "qpkna,pknb->qkab", left_side, column_block, preferred_element_type=jnp.float32
    )


def power_sum(column_block):
    return jnp.einsum(
        "pknb,pknb->kb", column_block, column_block, preferred_element_type=jnp.float32
    )


def normalize(visibility, row_power, column_power):
    scale_row = lax.rsqrt(row_power + epsilon)
    scale_column = lax.rsqrt(column_power + epsilon)
    return (visibility * scale_row[None, :, :, None] * scale_column[None, :, None, :]).astype(
        jnp.bfloat16
    )


def per_device(samples, fir_taps, station_order):
    tap_count = fir_taps.shape[0]
    channels = fir_taps.shape[1]
    stations_local = samples.shape[1]
    spectra_local = samples.shape[2] // channels
    stations = station_order.shape[0]
    frames = samples.reshape(2, stations_local, spectra_local, channels)
    earlier = frames[:, :, spectra_local - (tap_count - 1) :, :].astype(jnp.bfloat16)
    earlier = passed_along(earlier, "blk", 1)
    extended = jnp.concatenate([earlier.astype(jnp.float32), frames.astype(jnp.float32)], axis=2)
    filtered = fir_taps[0] * extended[:, :, 0:spectra_local]
    for tap_index in range(1, tap_count):
        filtered = (
            filtered + fir_taps[tap_index] * extended[:, :, tap_index : tap_index + spectra_local]
        )
    filtered = filtered.astype(jnp.bfloat16)
    cosine_table, sine_table = dft_tables(channels)
    cosine_part = jnp.einsum(
        "kc,pasc->pksa", cosine_table, filtered, preferred_element_type=jnp.float32
    )
    sine_part = jnp.einsum(
        "kc,pasc->pksa", sine_table, filtered, preferred_element_type=jnp.float32
    )
    real_part = cosine_part[0] + sine_part[1]
    imag_part = cosine_part[1] - sine_part[0]
    spectra = (
        jnp.stack([real_part, imag_part])
        .astype(jnp.bfloat16)
        .reshape(2, channels, spectra_local * stations_local)
    )
    groups = lax.axis_size("stn")
    blocks = lax.axis_size("blk")
    row_count = stations // blocks
    turned = lax.all_to_all(spectra, "stn", split_axis=1, concat_axis=2, tiled=True)
    local_channels = turned.shape[1]
    turned = turned.reshape(2, local_channels, groups, spectra_local, stations_local)
    turned = turned.transpose(0, 1, 3, 2, 4).reshape(2, local_channels, spectra_local, stations)
    ordered = jnp.take(turned, station_order, axis=3)
    row_start = lax.axis_index("blk") * row_count
    shard_piece = lax.all_gather(ordered, "blk", axis=2, tiled=True)
    row_block = lax.dynamic_slice_in_dim(shard_piece, row_start, row_count, 3)
    visibility = correlate(row_block, shard_piece)
    column_power = power_sum(shard_piece)
    row_power = lax.dynamic_slice_in_dim(column_power, row_start, row_count, 1)
    return normalize(visibility, row_power, column_power)


def solution(mesh):
    placed = (P(None, "stn", "blk"), P(), P())
    return jax.shard_map(
        per_device,
        mesh=mesh,
        in_specs=placed,
        out_specs=P(None, "stn", "blk", None),
        check_vma=False,
    )
```

profile of v0, /device:TPU:1, one launch (start us, length us, event | category | flops | bytes accessed | tf_op | source)
XLA Modules:
  0.0 280.8 jit_solution(16764004634024205850)
XLA Ops:
  6.5 2.5 fusion.67
  9.0 0.1 copy.59
  9.2 4.0 %collective-permute-start = (bf16[2,8,7,1024]{3,2,1,0:T(8,128)(2,1)S(1)}, bf16[2,8,7,1024]{3,2,1,0:T(8,128)(2,1)S(1)}, u32[]{:S(2)}, u32[]{:S(2)}) collective-permute-start(bf16[2,8,7,1024]{3,2,1,0:T(8,128)(2,1)S(1)} %copy.59), channel_id=1, source_target_pairs={{0,1},{1,2},{2,3},{3,4},{4,5},{5,6},{6,7},{8,9},{9,10},{10,11},{11... | collective-permute-start | bytes 688136 | tf_op jit(solution)/shard_map/ppermute | solution.py:14
  13.1 0.0 copy-start
  13.1 1.2 copy.33
  14.4 0.0 copy-done
  14.4 2.0 collective-permute-done
  16.5 2.4 fusion.18
  18.9 16.6 %fusion.50 = f32[2,1024,32,8]{1,2,3,0:T(8,128)S(1)} fusion(bf16[2,8,32,1024]{3,2,1,0:T(8,128)(2,1)S(1)} %fusion.18), kind=kOutput, calls=%fused_computation.62 | convolution fusion | flops 1089470464 | bytes 3145728 | tf_op jit(solution)/shard_map/kc,pasc->pksa/dot_general | solution.py:66
  35.5 16.5 %fusion.53 = f32[2,1024,32,8]{1,2,3,0:T(8,128)S(1)} fusion(bf16[2,8,32,1024]{3,2,1,0:T(8,128)(2,1)S(1)} %fusion.18), kind=kOutput, calls=%fused_computation.63 | convolution fusion | flops 1089470464 | bytes 3145728 | tf_op jit(solution)/shard_map/kc,pasc->pksa/dot_general | solution.py:63
  52.1 0.5 fusion.57
  52.6 0.6 copy_bitcast_fusion
  53.2 0.1 pad_maximum_fusion.1
  53.3 0.0 copy-start.1
  53.3 2.0 copy.37
  55.3 21.5 %all-to-all-start = ((bf16[2,1024,256]{2,0,1:T(2,128)(2,1)}), bf16[2,1024,256]{2,0,1:T(2,128)(2,1)S(1)}, u32[]{:S(2)}, u32[]{:S(2)}) async-start(bf16[2,1024,256]{2,0,1:T(2,128)(2,1)} %copy.37), calls=%async_computation | async-start | bytes 2097152 | tf_op jit(solution)/shard_map/all_to_all | solution.py:79
  76.8 0.0 all-gather.2.cloned.1.call-start
  76.9 0.0 copy-done.1
  76.9 51.8 %all-to-all-done = bf16[2,1024,256]{2,0,1:T(2,128)(2,1)S(1)} async-done(((bf16[2,1024,256]{2,0,1:T(2,128)(2,1)}), bf16[2,1024,256]{2,0,1:T(2,128)(2,1)S(1)}, u32[]{:S(2)}, u32[]{:S(2)}) %all-to-all-start) | async-done | bytes 1048608 | tf_op jit(solution)/shard_map/all_to_all | solution.py:79
  128.7 0.1 copy.38
  128.8 1.4 copy.39
  130.3 7.7 %copy.55 = bf16[2,16,32,64,8]{2,1,4,3,0:T(8,128)(2,1)} copy(bf16[2,16,32,64,8]{3,4,2,1,0:T(8,128)(2,1)S(1)} %bitcast.63) | data formatting | bytes 2097152 | tf_op jit(solution)/shard_map/reshape | solution.py:82
  137.9 5.5 %gather_fusion = bf16[512,2,16,32]{3,2,1,0:T(8,128)(2,1)} fusion(bf16[2,16,32,512]{2,1,3,0:T(8,128)(2,1)} %bitcast.65, s32[1024]{0:T(1024)S(1)} %pad_clamp_fusion), kind=kCustom, calls=%fused_computation | custom fusion | bytes 2099200 | tf_op jit(solution)/shard_map/jit(_take)/gather | solution.py:83
  143.4 4.6 %select_bitcast_fusion = bf16[2,16,32,512]{2,1,0,3:T(8,128)(2,1)} fusion(bf16[512,2,16,32]{3,2,1,0:T(8,128)(2,1)} %gather_fusion, pred[512]{0:T(512)(128)(4,1)S(1)} %compare_and_fusion), kind=kLoop, calls=%fused_computation.20 | loop fusion | flops 524288 | bytes 2097664 | tf_op jit(solution)/shard_map/jit(_take)/select_n | solution.py:83
  148.0 6.0 %copy.42 = bf16[2,16,32,512]{3,1,0,2:T(8,128)(2,1)} copy(bf16[2,16,32,512]{2,1,0,3:T(8,128)(2,1)} %select_bitcast_fusion) | data formatting | bytes 2097152 | tf_op jit(solution)/shard_map/jit(_take)/select_n | solution.py:83
  154.0 0.0 all-gather.2.cloned.1.call-update
  154.1 96.0 %all-gather.2.cloned.1.call-done = bf16[2,16,256,512]{3,1,0,2:T(8,128)(2,1)} async-done(((bf16[2,16,32,512]{3,1,0,2:T(8,128)(2,1)}), bf16[2,16,256,512]{3,1,0,2:T(8,128)(2,1)}) %all-gather.2.cloned.1.call-update) | async-done | bytes 8388624 | tf_op jit(solution)/shard_map/all_gather | solution.py:85
  250.1 5.1 %fusion = f32[16,512]{1,0:T(8,128)S(1)} fusion(bf16[2,16,256,512]{3,1,0,2:T(8,128)(2,1)} %all-gather.2.cloned.1.call-done), kind=kLoop, calls=%fused_computation.2 | loop fusion | flops 12574720 | bytes 8421376 | tf_op jit(solution)/shard_map/pknb,pknb->kb/dot_general | solution.py:33
  255.1 0.1 add_rsqrt_fusion.1
  255.2 2.2 constant_dynamic-slice_fusion
  257.5 2.2 copy.60
  259.7 0.1 fusion.68
  259.7 0.1 maximum_bitcast_fusion
  259.8 12.6 %fusion.45 = bf16[2,16,64,512]{3,2,0,1:T(8,128)(2,1)S(1)} fusion(f32[16,512]{1,0:T(8,128)S(1)} %add_rsqrt_fusion, f32[16,64]{1,0:T(8,128)S(1)} %add_rsqrt_fusion.1, bf16[1,2,16,256,64]{3,4,1,0,2:T(8,128)(2,1)S(1)} %maximum_bitcast_fusion, bf16[1,2,16,256,64]{3,4,1,0,2:T(8,128)(2,1)S(1)} %bitcast.66, bf16[2,16,256,512,1]{3,1,0,2,4:T(8,128)(2,1)} %bitcast.62), kind=kOutput, calls=%fused_computation.61 | convolution fusion | flops 1081081856 | bytes 12619776 | tf_op jit(solution)/shard_map/qpkna,pknb->qkab/dot_general | solution.py:27
  272.5 1.5 copy.45
  (7 shorter events, 0.1 us)
Async XLA Ops:
  9.2 7.3 %collective-permute-start = (bf16[2,8,7,1024]{3,2,1,0:T(8,128)(2,1)S(1)}, bf16[2,8,7,1024]{3,2,1,0:T(8,128)(2,1)S(1)}, u32[]{:S(2)}, u32[]{:S(2)}) collective-permute-start(bf16[2,8,7,1024]{3,2,1,0:T(8,128)(2,1)S(1)} %copy.59), channel_id=1, source_target_pairs={{0,1},{1,2},{2,3},{3,4},{4,5},{5,6},{6,7},{8,9},{9,10},{10,11},{11... | collective-permute-start | bytes 688136 | tf_op jit(solution)/shard_map/ppermute | solution.py:14
  13.1 1.2 copy-start
  53.3 23.6 %copy-start.1 = (s32[512]{0:T(512)S(1)}, s32[512]{0:T(512)}, u32[]{:S(2)}) copy-start(s32[512]{0:T(512)} %param.5) | copy-start | bytes 6148
  55.3 73.3 %all-to-all-start = ((bf16[2,1024,256]{2,0,1:T(2,128)(2,1)}), bf16[2,1024,256]{2,0,1:T(2,128)(2,1)S(1)}, u32[]{:S(2)}, u32[]{:S(2)}) async-start(bf16[2,1024,256]{2,0,1:T(2,128)(2,1)} %copy.37), calls=%async_computation | async-start | bytes 2097152 | tf_op jit(solution)/shard_map/all_to_all | solution.py:79
  76.8 173.2 %all-gather.2.cloned.1.call-start = ((), (), s32[]{:S(2)}) async-start(), calls=%async_computation.1 | async-start | bytes 9437184 | tf_op jit(solution)/shard_map/all_gather | solution.py:85
Sparse Core Ops, SparseCore 0:
  154.2 95.8 all-gather.1
where the time goes:
time: 281 us
  waiting for transfers between devices  150 us (53%)
  matrix products  45.8 us (16%)
  local copies, waits for them, and re-layouts  30.6 us (11%)
  starting transfers between devices  25.5 us (9%)
  other arithmetic  15.5 us (6%)
  between operations  13.6 us (5%)
    all_gather x1, waiting for transfers between devices, per_device(): shard_piece = lax.all_gather(ordered, 'blk', axis=2, tiled=True)  96 us
    all_to_all x1, waiting for transfers between devices, per_device(): lax.all_to_all(spectra, 'stn', split_axis=1, concat_axis=2, tiled=True)  51.8 us
    all_to_all x1, starting transfers between devices, per_device(): lax.all_to_all(spectra, 'stn', split_axis=1, concat_axis=2, tiled=True)  21.5 us
    dot_general x1, matrix products, per_device(): jnp.einsum('kc,pasc->pksa', sine_table, filtered, preferred_element_type=...  16.6 us
    dot_general x1, matrix products, per_device(): jnp.einsum('kc,pasc->pksa', cosine_table, filtered, preferred_element_typ...  16.5 us
    dot_general x1, matrix products, correlate(): jnp.einsum('qpkna,pknb->qkab', left_side, column_block, preferred_element...  12.6 us
    reshape x1, local copies, waits for them, and re-layouts, per_device(): turned.transpose(0, 1, 3, 2, 4)  7.65 us
    select_n x1, local copies, waits for them, and re-layouts, per_device(): ordered = jnp.take(turned, station_order, axis=3)  6.03 us
  transfers between devices with their start and end apart: 3, of which 3 were waited for; matrix products, arithmetic and copies ran while one was open for 0% of the time, Pallas kernels for 0%

commit v1 on v0

v1 whole, which is shorter than its diff:
```python
import functools
import math

import jax
import jax.numpy as jnp
from jax import lax
from jax.experimental import pallas as pl
from jax.experimental.pallas import tpu as pltpu
from jax.sharding import PartitionSpec as P

epsilon = 1e-06
MESH = pl.DeviceIdType.MESH


def passed_along(value, axis, steps):
    count = lax.axis_size(axis)
    initial, last = (max(0, -steps), min(count, count - steps))
    return lax.ppermute(value, axis, [(source, source + steps) for source in range(initial, last)])


def dft_tables(channels):
    channel_index = jnp.arange(channels, dtype=jnp.int32)
    phase_index = channel_index[:, None] * channel_index[None, :] % channels
    angle_table = phase_index.astype(jnp.float32) * (2.0 * math.pi / channels)
    return (jnp.cos(angle_table).astype(jnp.bfloat16), jnp.sin(angle_table).astype(jnp.bfloat16))


def exchange_kernel(axis, count, in_ref, out_ref, send_sem, recv_sem, own_sem):
    me = lax.axis_index(axis)
    barrier = pltpu.get_barrier_semaphore()

    def greet(step, carry):
        pl.semaphore_signal(
            barrier, inc=1, device_id={axis: lax.rem(me + step, count)}, device_id_type=MESH
        )
        return carry

    lax.fori_loop(1, count, greet, 0)
    own = pltpu.make_async_copy(in_ref.at[me], out_ref.at[me], own_sem)
    own.start()
    pl.semaphore_wait(barrier, count - 1)

    def send(step, carry):
        target = lax.rem(me + step, count)
        pltpu.make_async_remote_copy(
            src_ref=in_ref.at[target],
            dst_ref=out_ref.at[me],
            send_sem=send_sem,
            recv_sem=recv_sem,
            device_id={axis: target},
            device_id_type=MESH,
        ).start()
        return carry

    lax.fori_loop(1, count, send, 0)
    others = pl.ds(0, count - 1)
    pltpu.make_async_copy(in_ref.at[others], out_ref.at[others], recv_sem).wait()
    pltpu.make_async_copy(in_ref.at[others], out_ref.at[others], send_sem).wait()
    own.wait()


def exchange(blocks, axis, identity):
    count = lax.axis_size(axis)
    shape = blocks.shape
    flat = blocks.reshape(count, -1, 128)
    flat = pl.pallas_call(
        functools.partial(exchange_kernel, axis, count),
        out_shape=jax.ShapeDtypeStruct(flat.shape, flat.dtype),
        in_specs=[pl.BlockSpec(memory_space=pltpu.VMEM)],
        out_specs=pl.BlockSpec(memory_space=pltpu.VMEM),
        scratch_shapes=[pltpu.SemaphoreType.DMA] * 3,
        compiler_params=pltpu.CompilerParams(
            collective_id=identity, has_side_effects=True, vmem_limit_bytes=32 << 20
        ),
    )(flat)
    return flat.reshape(shape)


def per_device(samples, fir_taps, station_order):
    tap_count = fir_taps.shape[0]
    channels = fir_taps.shape[1]
    stations_local = samples.shape[1]
    spectra_local = samples.shape[2] // channels
    stations = station_order.shape[0]
    groups = lax.axis_size("stn")
    blocks = lax.axis_size("blk")
    per_group = channels // groups
    per_owner = per_group // blocks
    frames = samples.reshape(2, stations_local, spectra_local, channels)
    earlier = frames[:, :, spectra_local - (tap_count - 1) :, :].astype(jnp.bfloat16)
    earlier = passed_along(earlier, "blk", 1)
    extended = jnp.concatenate([earlier.astype(jnp.float32), frames.astype(jnp.float32)], axis=2)
    filtered = fir_taps[0] * extended[:, :, 0:spectra_local]
    for tap_index in range(1, tap_count):
        filtered = (
            filtered + fir_taps[tap_index] * extended[:, :, tap_index : tap_index + spectra_local]
        )
    filtered = filtered.astype(jnp.bfloat16)
    cosine_table, sine_table = dft_tables(channels)
    cosine_part = jnp.einsum(
        "kc,pasc->pksa", cosine_table, filtered, preferred_element_type=jnp.float32
    )
    sine_part = jnp.einsum(
        "kc,pasc->pksa", sine_table, filtered, preferred_element_type=jnp.float32
    )
    real_part = cosine_part[0] + sine_part[1]
    imag_part = cosine_part[1] - sine_part[0]
    spectra = jnp.stack([real_part, imag_part]).astype(jnp.bfloat16)
    spectra = spectra.reshape(2, groups, per_group, spectra_local, stations_local)
    turned = exchange(spectra.transpose(1, 0, 2, 3, 4), "stn", 0)
    turned = turned.reshape(groups, 2, blocks, per_owner, spectra_local, stations_local)
    owned = exchange(turned.transpose(2, 1, 3, 4, 0, 5), "blk", 1)
    owned = owned.reshape(blocks, 2, per_owner, spectra_local, stations)
    chosen = (station_order[None, :] == jnp.arange(stations)[:, None]).astype(jnp.bfloat16)
    ordered = jnp.einsum("bpkns,sr->bpknr", owned, chosen, preferred_element_type=jnp.bfloat16)
    swapped = jnp.stack([ordered[:, 1], -ordered[:, 0]], axis=1)
    left_side = jnp.stack([ordered, swapped])
    visibility = jnp.einsum(
        "qbpkna,bpknc->qkac", left_side, ordered, preferred_element_type=jnp.float32
    )
    power = jnp.einsum("bpkna,bpkna->ka", ordered, ordered, preferred_element_type=jnp.float32)
    scale = lax.rsqrt(power + epsilon)
    coherence = (visibility * scale[None, :, :, None] * scale[None, :, None, :]).astype(
        jnp.bfloat16
    )
    rows = stations // blocks
    coherence = coherence.reshape(2, per_owner, blocks, rows, stations).transpose(2, 0, 1, 3, 4)
    placed = exchange(coherence, "blk", 2)
    return placed.transpose(1, 0, 2, 3, 4).reshape(2, per_group, rows, stations)


def solution(mesh):
    placed = (P(None, "stn", "blk"), P(), P())
    return jax.shard_map(
        per_device,
        mesh=mesh,
        in_specs=placed,
        out_specs=P(None, "stn", "blk", None),
        check_vma=False,
    )
```

time: 281 us -> 230 us (0.82)
  waiting for transfers between devices: 150 us -> 2 us
  Pallas kernels: 0 us -> 119 us
  local copies, waits for them, and re-layouts: 30.6 us -> 57.4 us
  starting transfers between devices: 25.5 us -> 3.96 us
  between operations: 13.6 us -> 0.25 us
  matrix products: 45.8 us -> 35.2 us
  other arithmetic: 15.5 us -> 10.5 us
    pallas_call x0 -> x3, Pallas kernels: none -> 119 us  [exchange(): pl.pallas_call(functools.partial(exchange_kernel, axis, count), out_shape...]
    all_gather x1 -> x0, waiting for transfers between devices: 96 us -> none  [per_device(): shard_piece = lax.all_gather(ordered, 'blk', axis=2, tiled=True)]
    all_to_all x1 -> x0, waiting for transfers between devices: 51.8 us -> none  [per_device(): lax.all_to_all(spectra, 'stn', split_axis=1, concat_axis=2, tiled=True)]
    reshape x1 -> x5, local copies, waits for them, and re-layouts: 7.65 us -> 29.4 us  [the longest x3 24.8 us: exchange(): flat = blocks.reshape(count, -1, 128)]
    all_to_all x1 -> x0, starting transfers between devices: 21.5 us -> none  [per_device(): lax.all_to_all(spectra, 'stn', split_axis=1, concat_axis=2, tiled=True)]
    transpose x0 -> x3, local copies, waits for them, and re-layouts: none -> 19.1 us  [the longest x1 11 us: per_device(): owned = exchange(turned.transpose(2, 1, 3, 4, 0, 5), 'blk', 1)]
    dot_general x1 -> x2, matrix products: 12.6 us -> 2.07 us  [the longest x1 1.3 us: per_device(): jnp.einsum('qbpkna,bpknc->qkac', left_side, ordered, preferred_element_ty...]
    select_n x1 -> x0, local copies, waits for them, and re-layouts: 6.03 us -> none  [per_device(): ordered = jnp.take(turned, station_order, axis=3)]
  transfers between devices with their start and end apart: 3 -> 1, of which waited for: 3 -> 1; matrix products, arithmetic and copies ran while one was open for 0% -> 1% of each run, Pallas kernels for 0% -> 0%
where the time goes in v1:
time: 230 us; the launch traced here: 229 us
  Pallas kernels  119 us (52%)
  local copies, waits for them, and re-layouts  57.4 us (25%)
  matrix products  35.2 us (15%)
  other arithmetic  10.5 us (5%)
  starting transfers between devices  3.96 us (2%)
    pallas_call x3, Pallas kernels, exchange(): pl.pallas_call(functools.partial(exchange_kernel, axis, count), out_shape...  119 us
    reshape x3, local copies, waits for them, and re-layouts, exchange(): flat = blocks.reshape(count, -1, 128)  24.8 us
    dot_general x1, matrix products, per_device(): jnp.einsum('kc,pasc->pksa', sine_table, filtered, preferred_element_type=...  16.6 us
    dot_general x1, matrix products, per_device(): jnp.einsum('kc,pasc->pksa', cosine_table, filtered, preferred_element_typ...  16.5 us
    transpose x1, local copies, waits for them, and re-layouts, per_device(): owned = exchange(turned.transpose(2, 1, 3, 4, 0, 5), 'blk', 1)  11 us
    transpose x1, local copies, waits for them, and re-layouts, per_device(): turned = exchange(spectra.transpose(1, 0, 2, 3, 4), 'stn', 0)  6.59 us
  transfers between devices with their start and end apart: 1, of which 1 were waited for; matrix products, arithmetic and copies ran while one was open for 1% of the time, Pallas kernels for 0%

profile of v1, /device:TPU:1, one launch (start us, length us, event | category | flops | bytes accessed | tf_op | source)
XLA Modules:
  0.0 228.7 jit_solution(12134650849404779319)
XLA Ops:
  0.0 2.5 %fusion.61 = (bf16[2,8,32768]{2,1,0:T(8,128)(2,1)S(1)}, f32[2,8,32768]{2,1,0:T(8,128)S(1)}) fusion(s32[2,8,32768]{2,1,0:T(8,128)} %param.3), kind=kLoop, calls=%fused_computation.81 | loop fusion | flops 1048576 | bytes 5242880 | tf_op jit(solution)/shard_map/convert.4
  2.5 0.1 copy.42
  2.6 4.0 %collective-permute-start = (bf16[2,8,7,1024]{3,2,1,0:T(8,128)(2,1)S(1)}, bf16[2,8,7,1024]{3,2,1,0:T(8,128)(2,1)S(1)}, u32[]{:S(2)}, u32[]{:S(2)}) collective-permute-start(bf16[2,8,7,1024]{3,2,1,0:T(8,128)(2,1)S(1)} %copy.42), channel_id=1, source_target_pairs={{0,1},{1,2},{2,3},{3,4},{4,5},{5,6},{6,7},{8,9},{9,10},{10,11},{11... | collective-permute-start | bytes 688136 | tf_op jit(solution)/shard_map/ppermute | solution.py:18
  6.6 0.0 copy-start.1
  6.6 1.2 copy.15
  7.8 0.0 copy-done.1
  7.9 2.0 collective-permute-done
  9.9 2.4 %fusion.13 = bf16[2,8,32,1024]{3,2,1,0:T(8,128)(2,1)S(1)} fusion(f32[2,8,32,1024]{3,2,1,0:T(8,128)S(1)} %copy.15, f32[2,8,7,1024]{3,2,1,0:T(8,128)S(1)} %convert_element_type.30, f32[1024]{0:T(1024)S(1)} %bitcast.90, f32[1024]{0:T(1024)S(1)} %bitcast.91, f32[1024]{0:T(1024)S(1)} %bitcast.85, f32[1024]{0:T(1024)S(1)} %bitcast.86, f32[1024]{0:T(1024)S(1)} %bitcast.87, ...), kind=kLoop, calls=%fused_computation.32 | loop fusion | flops 12058624 | bytes 3637248 | tf_op jit(solution)/shard_map/convert_element_type | solution.py:98
  12.3 16.6 %fusion.40 = f32[2,1024,32,8]{1,2,3,0:T(8,128)S(1)} fusion(bf16[2,8,32,1024]{3,2,1,0:T(8,128)(2,1)S(1)} %fusion.13), kind=kOutput, calls=%fused_computation.59 | convolution fusion | flops 1089470464 | bytes 3145728 | tf_op jit(solution)/shard_map/kc,pasc->pksa/dot_general | solution.py:103
  29.0 16.5 %fusion.43 = f32[2,1024,32,8]{1,2,3,0:T(8,128)S(1)} fusion(bf16[2,8,32,1024]{3,2,1,0:T(8,128)(2,1)S(1)} %fusion.13), kind=kOutput, calls=%fused_computation.60 | convolution fusion | flops 1089470464 | bytes 3145728 | tf_op jit(solution)/shard_map/kc,pasc->pksa/dot_general | solution.py:100
  45.5 0.5 fusion.47
  46.1 1.6 copy.17
  47.7 2.5 %copy.18 = bf16[1,1024,32,8]{2,3,1,0:T(8,128)(2,1)} copy(bf16[1,1024,32,8]{1,2,3,0:T(8,128)(2,1)S(1)} %get-tuple-element.6) | data formatting | bytes 1048576 | tf_op jit(solution)/shard_map/convert.2
  50.2 4.5 %maximum_bitcast_fusion = bf16[64,2,16,32,8]{3,4,2,0,1:T(8,128)(2,1)} fusion(bf16[1,64,16,32,8]{3,4,2,1,0:T(8,128)(2,1)} %bitcast.78, bf16[1,64,16,32,8]{3,4,2,1,0:T(8,128)(2,1)S(1)} %bitcast.77), kind=kLoop, calls=%fused_computation.12 | loop fusion | flops 524288 | bytes 2097152 | tf_op jit(solution)/shard_map/transpose | solution.py:110
  54.7 6.6 %copy.19 = bf16[64,2,16,32,8]{0,4,3,2,1:T(8,128)(2,1)S(1)} copy(bf16[64,2,16,32,8]{3,4,2,0,1:T(8,128)(2,1)} %maximum_bitcast_fusion) | data formatting | bytes 2097152 | tf_op jit(solution)/shard_map/transpose | solution.py:110
  61.2 1.7 copy.20.in_ref
  62.9 67.2 %shard_map.37 = bf16[64,64,128]{2,1,0:T(8,128)(2,1)S(1)} custom-call(bf16[64,64,128]{2,1,0:T(8,128)(2,1)S(1)} %copy.20.in_ref), custom_call_target="tpu_custom_call" | custom-call | tf_op jit(solution)/shard_map/pallas_call | solution.py:66
  130.1 1.5 copy.21
  131.6 11.0 %copy.22 = bf16[8,2,2,32,64,8]{5,4,3,2,1,0:T(8,128)(2,1)} copy(bf16[8,2,2,32,64,8]{4,5,3,2,0,1:T(8,128)(2,1)S(1)} %bitcast.75) | data formatting | bytes 2097152 | tf_op jit(solution)/shard_map/transpose | solution.py:112
  142.6 20.0 %reshape.39.in_ref = bf16[8,512,128]{2,1,0:T(8,128)(2,1)S(1)} reshape(bf16[8,2,2,32,64,8]{5,4,3,2,1,0:T(8,128)(2,1)} %copy.22) | data formatting | bytes 2097152 | tf_op jit(solution)/shard_map/reshape | solution.py:65
  162.6 0.0 copy-start.2
  162.6 19.2 %shard_map.38 = bf16[8,512,128]{2,1,0:T(8,128)(2,1)S(1)} custom-call(bf16[8,512,128]{2,1,0:T(8,128)(2,1)S(1)} %reshape.39.in_ref), custom_call_target="tpu_custom_call" | custom-call | tf_op jit(solution)/shard_map/pallas_call | solution.py:66
  181.9 0.7 reshape_reshape.7
  182.6 0.0 copy-done.2
  182.6 0.8 fusion.35
  183.4 0.1 fusion.62
  183.4 0.1 maximum_bitcast_fusion.1
  183.5 1.3 fusion.36
  184.8 0.4 fusion.4
  185.3 1.5 copy.49
  186.8 3.1 %reshape.41.in_ref = bf16[8,1024,128]{2,1,0:T(8,128)(2,1)S(1)} reshape(bf16[8,2,2,64,512]{4,3,2,1,0:T(8,128)(2,1)} %bitcast.80) | data formatting | bytes 4194304 | tf_op jit(solution)/shard_map/reshape | solution.py:65
  189.9 32.9 %shard_map.39 = bf16[8,1024,128]{2,1,0:T(8,128)(2,1)S(1)} custom-call(bf16[8,1024,128]{2,1,0:T(8,128)(2,1)S(1)} %reshape.41.in_ref), custom_call_target="tpu_custom_call" | custom-call | tf_op jit(solution)/shard_map/pallas_call | solution.py:66
  222.7 0.0 copy-start
  222.8 1.3 copy-done
  224.1 3.1 %reshape.42 = bf16[8,2,2,64,512]{4,3,2,1,0:T(8,128)(2,1)S(1)} reshape(bf16[8,1024,128]{2,1,0:T(8,128)(2,1)} %copy-done) | data formatting | bytes 4194304 | tf_op jit(solution)/shard_map/reshape | solution.py:76
  227.2 1.5 copy.26
  (4 shorter events, 0.1 us)
Async XLA Ops:
  2.6 7.3 %collective-permute-start = (bf16[2,8,7,1024]{3,2,1,0:T(8,128)(2,1)S(1)}, bf16[2,8,7,1024]{3,2,1,0:T(8,128)(2,1)S(1)}, u32[]{:S(2)}, u32[]{:S(2)}) collective-permute-start(bf16[2,8,7,1024]{3,2,1,0:T(8,128)(2,1)S(1)} %copy.42), channel_id=1, source_target_pairs={{0,1},{1,2},{2,3},{3,4},{4,5},{5,6},{6,7},{8,9},{9,10},{10,11},{11... | collective-permute-start | bytes 688136 | tf_op jit(solution)/shard_map/ppermute | solution.py:18
  6.6 1.2 copy-start.1
  162.6 19.9 %copy-start.2 = (s32[512]{0:T(512)S(1)}, s32[512]{0:T(512)}, u32[]{:S(2)}) copy-start(s32[512]{0:T(512)} %param.5) | copy-start | bytes 6148
  222.7 1.3 copy-start

commit v2 on v0

v2 whole, which is shorter than its diff:
```python
import functools

import jax
import jax.numpy as jnp
import ml_dtypes
import numpy as np
from jax import lax
from jax.experimental import pallas as pl
from jax.experimental.pallas import tpu as pltpu
from jax.sharding import PartitionSpec as P

epsilon = 1e-06
MESH = pl.DeviceIdType.MESH
F32 = jnp.float32
BF16 = jnp.bfloat16
GROUPS = 64
BLOCKS = 8
TAPS = 8
CHANNELS = 1024
STATIONS = 512
LOCAL = 8
HALF = 16


@functools.cache
def transform_table():
    index = np.arange(CHANNELS, dtype=np.int64)
    angle = (index[:, None] * index[None, :] % CHANNELS) * (2.0 * np.pi / CHANNELS)
    cosine = np.cos(angle).astype(np.float32)
    sine = np.sin(angle).astype(np.float32)
    rows = np.stack(
        [np.concatenate([cosine, sine], axis=1), np.concatenate([-sine, cosine], axis=1)]
    ).astype(ml_dtypes.bfloat16)
    rows = rows.reshape(2, GROUPS, BLOCKS, 2, 2 * CHANNELS).transpose(3, 1, 0, 2, 4)
    return np.ascontiguousarray(rows.reshape(2, CHANNELS * 2 // 2, 2 * CHANNELS))


def dot(a, b):
    return jnp.dot(a, b, preferred_element_type=F32)


def kernel(
    samples_ref, taps_ref, order_ref, table_ref, out_ref,
    frames, table, edge_out, edge_in, lined, filtered,
    sent, got, turned, blocks, lanes, swap, chosen, ordered, crossed, ordered_t, vis, col_scale,
    row_scale, done,
    load_sem, edge_sem, z_send, z_recv, x_send, x_recv, o_send, o_recv, own_sem,
):
    s = lax.axis_index("stn")
    b = lax.axis_index("blk")
    barrier = pltpu.get_barrier_semaphore()

    def greet_group(step, carry):
        pl.semaphore_signal(
            barrier, inc=1, device_id=(lax.rem(s + step, GROUPS), b), device_id_type=MESH
        )
        return carry

    def greet_block(step, carry):
        pl.semaphore_signal(
            barrier, inc=1, device_id=(s, lax.rem(b + step, BLOCKS)), device_id_type=MESH
        )
        return carry

    load_frames = pltpu.make_async_copy(samples_ref, frames, load_sem.at[0])
    load_frames.start()
    load_tables = [
        pltpu.make_async_copy(table_ref.at[c], table.at[c], load_sem.at[1 + c]) for c in range(2)
    ]
    for load in load_tables:
        load.start()
    lax.fori_loop(1, BLOCKS, greet_block, 0)
    lax.fori_loop(1, GROUPS, greet_group, 0)

    load_frames.wait()
    for t in range(TAPS - 1):
        place = (32 - (TAPS - 1) + t) * CHANNELS
        edge_out[t] = jnp.concatenate(
            [frames[p, :, place : place + CHANNELS].astype(F32) for p in range(2)], axis=0
        ).astype(BF16)

    def filter_half(half):
        def one(block, carry):
            column = pl.multiple_of(block * 128, 128)
            taps = [
                jnp.broadcast_to(taps_ref[t : t + 1, pl.ds(column, 128)], (LOCAL, 128))
                for t in range(TAPS)
            ]
            for p in range(2):
                held = []
                for t in range(HALF * half - (TAPS - 1), HALF * half + HALF):
                    if t < 0:
                        value = edge_in[t + TAPS - 1, :, pl.ds(column, 128)].astype(F32)
                        held.append(value[LOCAL * p : LOCAL * (p + 1)])
                    else:
                        place = pl.multiple_of(t * CHANNELS + column, 128)
                        held.append(frames[p, :, pl.ds(place, 128)].astype(F32))
                for t in range(HALF):
                    total = taps[0] * held[t]
                    for j in range(1, TAPS):
                        total = total + taps[j] * held[t + j]
                    lined[p, LOCAL * t : LOCAL * (t + 1), :] = total
            for p in range(2):
                rows = jnp.concatenate(
                    [lined[p, pl.ds(a, HALF, stride=LOCAL), :] for a in range(LOCAL)], axis=0
                )
                place = pl.multiple_of(p * CHANNELS + column, 128)
                filtered[pl.ds(place, 128), 128 * half : 128 * (half + 1)] = rows.T.astype(BF16)
            return carry

        lax.fori_loop(0, CHANNELS // 128, one, 0)

    def send_group(c, half, block):
        def one(step, carry):
            target = block * 16 + lax.rem(lax.rem(s, 16) + step, 16)

            @pl.when(target != s)
            def _():
                pltpu.make_async_remote_copy(
                    src_ref=sent.at[c, half, target],
                    dst_ref=got.at[c, half, s],
                    send_sem=z_send.at[c, half],
                    recv_sem=z_recv.at[c, half],
                    device_id=(target, b),
                    device_id_type=MESH,
                ).start()

            return carry

        lax.fori_loop(0, 16, one, 0)

    def transform(c, halves):
        def one(step, carry):
            block = lax.rem(s // 16 + step, 4)
            rows = table[c, pl.ds(pl.multiple_of(block * 256, 256), 256), :]
            if len(halves) == 2:
                result = dot(rows, filtered[...])
            else:
                result = dot(rows, filtered[:, 128 * halves[0] : 128 * (halves[0] + 1)])
            for i, half in enumerate(halves):
                sent[c, half, pl.ds(block * 16, 16)] = (
                    result[:, 128 * i : 128 * (i + 1)].astype(BF16).reshape(16, 16, 128)
                )
            for half in halves:
                send_group(c, half, block)
            return carry

        lax.fori_loop(0, 4, one, 0)
        for half in halves:
            got[c, half, s] = sent[c, half, s]

    filter_half(1)
    pl.semaphore_wait(barrier, GROUPS - 1 + BLOCKS - 1)

    edge = pltpu.make_async_remote_copy(
        src_ref=edge_out,
        dst_ref=edge_in,
        send_sem=edge_sem.at[0],
        recv_sem=edge_sem.at[1],
        device_id=(s, lax.rem(b + 1, BLOCKS)),
        device_id_type=MESH,
    )

    @pl.when(b < BLOCKS - 1)
    def _():
        edge.start()

    load_tables[0].wait()
    transform(0, (1,))

    @pl.when(b == 0)
    def _():
        edge_in[...] = jnp.zeros_like(edge_in)

    @pl.when(b > 0)
    def _():
        edge.wait_recv()

    filter_half(0)
    transform(0, (0,))
    load_tables[1].wait()
    transform(1, (1, 0))

    row = lax.broadcasted_iota(jnp.int32, (256, 256), 0)
    column = lax.broadcasted_iota(jnp.int32, (256, 256), 1)
    matches = (row // 16 == column % 16) & (row % 16 == column // 16)
    swap[...] = jnp.where(matches, 1.0, 0.0).astype(BF16)
    for i in range(4):
        place = lax.broadcasted_iota(jnp.int32, (128, STATIONS), 0) + 128 * i
        station = (place % GROUPS) * LOCAL + place // GROUPS
        hot = jnp.where(station == order_ref[...], 1.0, 0.0)
        for j in range(4):
            chosen[128 * j : 128 * (j + 1), 128 * i : 128 * (i + 1)] = (
                hot[:, 128 * j : 128 * (j + 1)].T.astype(BF16)
            )

    def turn(c, half):
        others = pl.ds(0, GROUPS - 1)
        pltpu.make_async_copy(
            sent.at[c, half, others], got.at[c, half, others], z_recv.at[c, half]
        ).wait()
        for i in range(4):
            rows = got[c, half, 16 * i : 16 * (i + 1)].reshape(256, 128)
            rows = dot(swap[...], rows).astype(BF16).reshape(16, 16, 128)
            for x in range(16):
                turned[c, half, x % 8, x // 8, 16 * i : 16 * (i + 1), :] = rows[x]

        def one(step, carry):
            target = lax.rem(b + step, BLOCKS)
            pltpu.make_async_remote_copy(
                src_ref=turned.at[c, half, target],
                dst_ref=blocks.at[c, half, b],
                send_sem=x_send.at[c, half],
                recv_sem=x_recv.at[c, half],
                device_id=(s, target),
                device_id_type=MESH,
            ).start()
            return carry

        lax.fori_loop(1, BLOCKS, one, 0)
        blocks[c, half, b] = turned[c, half, b]

    def line_up(c, half):
        others = pl.ds(0, BLOCKS - 1)
        pltpu.make_async_copy(
            turned.at[c, half, others], blocks.at[c, half, others], x_recv.at[c, half]
        ).wait()
        lane = lax.broadcasted_iota(jnp.int32, (16, 128), 1) // 16

        def one(step, carry):
            first = pl.multiple_of(step * 16, 16)
            for p in range(2):
                held = [blocks[c, half, i, p, pl.ds(first, 16), :].astype(F32) for i in range(8)]
                for d in (1, 2, 4):
                    high = lane & d != 0
                    for i in range(8):
                        if i & d == 0:
                            low_part, high_part = held[i], held[i + d]
                            held[i] = jnp.where(
                                high, pltpu.roll(high_part, 16 * d, 1), low_part
                            )
                            held[i + d] = jnp.where(
                                high, high_part, pltpu.roll(low_part, 128 - 16 * d, 1)
                            )
                for i in range(8):
                    place = pl.multiple_of(i * GROUPS + first, 16)
                    column = 256 * p + 128 * half
                    lanes[pl.ds(place, 16), column : column + 128] = held[i].astype(BF16)
            return carry

        lax.fori_loop(0, GROUPS // 16, one, 0)

    def correlate(c):
        def choose(i, carry):
            rows = pl.ds(pl.multiple_of(i * 128, 128), 128)
            value = dot(chosen[rows, :], lanes[...])
            ordered[rows, :] = value.astype(BF16)
            crossed[rows, 0:256] = value[:, 256:512].astype(BF16)
            crossed[rows, 256:512] = (-value[:, 0:256]).astype(BF16)
            for j in range(4):
                ordered_t[128 * j : 128 * (j + 1), rows] = (
                    value[:, 128 * j : 128 * (j + 1)].T.astype(BF16)
                )
            return carry

        lax.fori_loop(0, 4, choose, 0)

        def multiply(i, carry):
            rows = pl.ds(pl.multiple_of(i * 128, 128), 128)
            vis[0, rows, :] = dot(ordered[rows, :], ordered_t[...])
            vis[1, rows, :] = dot(crossed[rows, :], ordered_t[...])
            return carry

        lax.fori_loop(0, 4, multiply, 0)
        same = lax.broadcasted_iota(jnp.int32, (128, 128), 0) == lax.broadcasted_iota(
            jnp.int32, (128, 128), 1
        )
        for i in range(4):
            rows = slice(128 * i, 128 * (i + 1))
            power = jnp.where(same, vis[0, rows, rows], 0.0)
            col_scale[rows, :] = lax.rsqrt(jnp.sum(power, axis=1, keepdims=True) + epsilon)
            row_scale[:, rows] = lax.rsqrt(jnp.sum(power, axis=0, keepdims=True) + epsilon)

        def finish(step, carry):
            target = lax.rem(b + step, BLOCKS)
            rows = pl.ds(pl.multiple_of(target * 64, 64), 64)
            scale = col_scale[rows, :] * row_scale[...]
            for q in range(2):
                done[c, target, q] = (vis[q, rows, :] * scale).astype(BF16)

            @pl.when(step < BLOCKS)
            def _():
                pltpu.make_async_remote_copy(
                    src_ref=done.at[c, target],
                    dst_ref=out_ref.at[:, 2 * b + c],
                    send_sem=o_send.at[c],
                    recv_sem=o_recv.at[c],
                    device_id=(s, target),
                    device_id_type=MESH,
                ).start()

            return carry

        lax.fori_loop(1, BLOCKS + 1, finish, 0)
        pltpu.make_async_copy(done.at[c, b], out_ref.at[:, 2 * b + c], own_sem.at[c]).start()

    for c in range(2):
        turn(c, 1)
        turn(c, 0)
        line_up(c, 1)
        line_up(c, 0)
        correlate(c)

    @pl.when(b < BLOCKS - 1)
    def _():
        edge.wait_send()

    group_others = pl.ds(0, GROUPS - 1)
    block_others = pl.ds(0, BLOCKS - 1)
    for c in range(2):
        for half in range(2):
            pltpu.make_async_copy(
                sent.at[c, half, group_others], got.at[c, half, group_others], z_send.at[c, half]
            ).wait()
            pltpu.make_async_copy(
                turned.at[c, half, block_others],
                blocks.at[c, half, block_others],
                x_send.at[c, half],
            ).wait()
        pltpu.make_async_copy(
            done.at[c, block_others], done.at[c, block_others], o_send.at[c]
        ).wait()
        pltpu.make_async_copy(
            done.at[c, block_others], done.at[c, block_others], o_recv.at[c]
        ).wait()
        pltpu.make_async_copy(done.at[c, b], out_ref.at[:, 2 * b + c], own_sem.at[c]).wait()


def per_device(samples, fir_taps, station_order):
    anywhere = pl.BlockSpec(memory_space=pl.ANY)
    near = pl.BlockSpec(memory_space=pltpu.VMEM)
    table = jnp.asarray(transform_table())
    dma = pltpu.SemaphoreType.DMA
    return pl.pallas_call(
        kernel,
        out_shape=jax.ShapeDtypeStruct((2, 16, 64, STATIONS), BF16),
        in_specs=[anywhere, near, near, anywhere],
        out_specs=anywhere,
        scratch_shapes=[
            pltpu.VMEM(samples.shape, jnp.int32),
            pltpu.VMEM(table.shape, BF16),
            pltpu.VMEM((TAPS - 1, 2 * LOCAL, CHANNELS), BF16),
            pltpu.VMEM((TAPS - 1, 2 * LOCAL, CHANNELS), BF16),
            pltpu.VMEM((2, 128, 128), F32),
            pltpu.VMEM((2 * CHANNELS, 256), BF16),
            pltpu.VMEM((2, 2, GROUPS, 16, 128), BF16),
            pltpu.VMEM((2, 2, GROUPS, 16, 128), BF16),
            pltpu.VMEM((2, 2, BLOCKS, 2, GROUPS, 128), BF16),
            pltpu.VMEM((2, 2, BLOCKS, 2, GROUPS, 128), BF16),
            pltpu.VMEM((STATIONS, STATIONS), BF16),
            pltpu.VMEM((256, 256), BF16),
            pltpu.VMEM((STATIONS, STATIONS), BF16),
            pltpu.VMEM((STATIONS, STATIONS), BF16),
            pltpu.VMEM((STATIONS, STATIONS), BF16),
            pltpu.VMEM((STATIONS, STATIONS), BF16),
            pltpu.VMEM((2, STATIONS, STATIONS), F32),
            pltpu.VMEM((STATIONS, 1), F32),
            pltpu.VMEM((1, STATIONS), F32),
            pltpu.VMEM((2, BLOCKS, 2, 64, STATIONS), BF16),
            dma((3,)),
            dma((2,)),
            dma((2, 2)),
            dma((2, 2)),
            dma((2, 2)),
            dma((2, 2)),
            dma((2,)),
            dma((2,)),
            dma((2,)),
        ],
        compiler_params=pltpu.CompilerParams(
            collective_id=0, has_side_effects=True, vmem_limit_bytes=48 << 20
        ),
        cost_estimate=pl.CostEstimate(
            flops=4_000_000_000, bytes_accessed=14_000_000, transcendentals=2048
        ),
    )(samples, fir_taps, station_order.reshape(1, STATIONS), table)


def solution(mesh):
    placed = (P(None, "stn", "blk"), P(), P())
    return jax.shard_map(
        per_device,
        mesh=mesh,
        in_specs=placed,
        out_specs=P(None, "stn", "blk", None),
        check_vma=False,
    )
```

time: 281 us -> 99 us (0.35)
  waiting for transfers between devices: 150 us -> 0 us
  Pallas kernels: 0 us -> 94.4 us
  matrix products: 45.8 us -> 0 us
  local copies, waits for them, and re-layouts: 30.6 us -> 4.35 us
  starting transfers between devices: 25.5 us -> 0 us
  other arithmetic: 15.5 us -> 0 us
  between operations: 13.6 us -> 0.01 us
    all_gather x1 -> x0, waiting for transfers between devices: 96 us -> none  [per_device(): shard_piece = lax.all_gather(ordered, 'blk', axis=2, tiled=True)]
    pallas_call x0 -> x1, Pallas kernels: none -> 94.4 us  [per_device(): pl.pallas_call(kernel, out_shape=jax.ShapeDtypeStruct((2, 16, 64, STATION...]
    all_to_all x1 -> x0, waiting for transfers between devices: 51.8 us -> none  [per_device(): lax.all_to_all(spectra, 'stn', split_axis=1, concat_axis=2, tiled=True)]
    dot_general x3 -> x0, matrix products: 45.8 us -> none  [the longest x1 16.6 us: per_device(): jnp.einsum('kc,pasc->pksa', sine_table, filtered, preferred_element_type=...]
    all_to_all x1 -> x0, starting transfers between devices: 21.5 us -> none  [per_device(): lax.all_to_all(spectra, 'stn', split_axis=1, concat_axis=2, tiled=True)]
    reshape x1 -> x0, local copies, waits for them, and re-layouts: 7.65 us -> none  [per_device(): turned.transpose(0, 1, 3, 2, 4)]
    select_n x1 -> x0, local copies, waits for them, and re-layouts: 6.03 us -> none  [per_device(): ordered = jnp.take(turned, station_order, axis=3)]
    gather x1 -> x0, local copies, waits for them, and re-layouts: 5.51 us -> none  [per_device(): ordered = jnp.take(turned, station_order, axis=3)]
  transfers between devices with their start and end apart: 3 -> 0, of which waited for: 3 -> 0; matrix products, arithmetic and copies ran while one was open for 0% -> 0% of each run, Pallas kernels for 0% -> 0%
where the time goes in v2:
time: 99 us; the launch traced here: 98.8 us
  Pallas kernels  94.4 us (95%)
  local copies, waits for them, and re-layouts  4.35 us (4%)
    pallas_call x1, Pallas kernels, per_device(): pl.pallas_call(kernel, out_shape=jax.ShapeDtypeStruct((2, 16, 64, STATION...  94.4 us
    unnamed x7, local copies, waits for them, and re-layouts  4.35 us

profile of v2, /device:TPU:1, one launch (start us, length us, event | category | flops | bytes accessed | tf_op | source)
XLA Modules:
  0.0 98.8 jit_solution(15294108326055017958)
XLA Ops:
  0.0 0.0 copy-start
  0.0 1.6 %copy-done = s32[2,8,32768]{2,1,0:T(8,128)S(1)} copy-done((s32[2,8,32768]{2,1,0:T(8,128)S(1)}, s32[2,8,32768]{2,1,0:T(8,128)}, u32[]{:S(2)}) %copy-start) | copy-done | bytes 2097176
  1.6 0.0 copy-start.1
  1.6 0.8 copy-done.1
  2.4 0.0 copy-start.2
  2.4 0.7 copy-done.2
  3.0 94.4 %shard_map.46 = bf16[2,16,64,512]{3,2,1,0:T(8,128)(2,1)S(1)} custom-call(s32[2,8,32768]{2,1,0:T(8,128)S(1)} %copy-done, f32[8,1024]{1,0:T(8,128)S(1)} %copy-done.1, s32[1,512]{1,0:T(1,128)S(1)} %bitcast.1, bf16[2,1024,2048]{2,1,0:T(8,128)(2,1)} %constant.2.clone.table_ref), custom_call_target="tpu_custom_call" | custom-call | flops 4000000000 | bytes 14000000 | tf_op jit(solution)/shard_map/pallas_call | solution.py:344
  97.5 1.3 %copy.6 = bf16[2,16,64,512]{3,2,1,0:T(8,128)(2,1)} copy(bf16[2,16,64,512]{3,2,1,0:T(8,128)(2,1)S(1)} %shard_map.46) | data formatting | bytes 4194304
Async XLA Ops:
  0.0 1.6 %copy-start = (s32[2,8,32768]{2,1,0:T(8,128)S(1)}, s32[2,8,32768]{2,1,0:T(8,128)}, u32[]{:S(2)}) copy-start(s32[2,8,32768]{2,1,0:T(8,128)} %samples_ref.1) | copy-start | bytes 6291460
  1.6 0.8 copy-start.1
  2.4 0.7 copy-start.2

commit v3 on v2

--- a/solution.py
+++ b/solution.py
@@ -40,10 +40,10 @@
 
 
 def kernel(
-    samples_ref, taps_ref, order_ref, table_ref, out_ref,
-    frames, table, edge_out, edge_in, lined, filtered,
-    sent, got, turned, blocks, lanes, swap, chosen, ordered, crossed, ordered_t, vis, col_scale,
-    row_scale, done,
+    samples_ref, taps_in, order_in, table_ref, out_ref,
+    frames, taps_ref, order_ref, table, edge_out, edge_in, lined, filtered,
+    sent, got, turned, blocks, lanes, swap, chosen, pair, ordered_t, power, col_scale,
+    row_scale, done, mixed,
     load_sem, edge_sem, z_send, z_recv, x_send, x_recv, o_send, o_recv, own_sem,
 ):
     s = lax.axis_index("stn")
@@ -62,17 +62,24 @@
         )
         return carry
 
-    load_frames = pltpu.make_async_copy(samples_ref, frames, load_sem.at[0])
-    load_frames.start()
-    load_tables = [
-        pltpu.make_async_copy(table_ref.at[c], table.at[c], load_sem.at[1 + c]) for c in range(2)
+    lax.fori_loop(1, GROUPS, greet_group, 0)
+    lax.fori_loop(1, BLOCKS, greet_block, 0)
+    loads = [
+        pltpu.make_async_copy(source, target, load_sem.at[i])
+        for i, (source, target) in enumerate(
+            [
+                (taps_in, taps_ref),
+                (samples_ref, frames),
+                (table_ref.at[0], table.at[0]),
+                (table_ref.at[1], table.at[1]),
+                (order_in, order_ref),
+            ]
+        )
     ]
-    for load in load_tables:
+    for load in loads:
         load.start()
-    lax.fori_loop(1, BLOCKS, greet_block, 0)
-    lax.fori_loop(1, GROUPS, greet_group, 0)
-
-    load_frames.wait()
+    loads[0].wait()
+    loads[1].wait()
     for t in range(TAPS - 1):
         place = (32 - (TAPS - 1) + t) * CHANNELS
         edge_out[t] = jnp.concatenate(
@@ -110,24 +117,26 @@
 
         lax.fori_loop(0, CHANNELS // 128, one, 0)
 
-    def send_group(c, half, block):
+    def send(c, half, target):
+        pltpu.make_async_remote_copy(
+            src_ref=sent.at[c, half, target],
+            dst_ref=got.at[c, half, s],
+            send_sem=z_send.at[c, half],
+            recv_sem=z_recv.at[c, half],
+            device_id=(target, b),
+            device_id_type=MESH,
+        ).start()
+
+    def send_all(c, half):
+        send(c, half, lax.rem(s + GROUPS // 2, GROUPS))
+
         def one(step, carry):
-            target = block * 16 + lax.rem(lax.rem(s, 16) + step, 16)
-
-            @pl.when(target != s)
-            def _():
-                pltpu.make_async_remote_copy(
-                    src_ref=sent.at[c, half, target],
-                    dst_ref=got.at[c, half, s],
-                    send_sem=z_send.at[c, half],
-                    recv_sem=z_recv.at[c, half],
-                    device_id=(target, b),
-                    device_id_type=MESH,
-                ).start()
-
-            return carry
-
-        lax.fori_loop(0, 16, one, 0)
+            offset = GROUPS // 2 - step
+            send(c, half, lax.rem(s + offset, GROUPS))
+            send(c, half, lax.rem(s + GROUPS - offset, GROUPS))
+            return carry
+
+        lax.fori_loop(1, GROUPS // 2, one, 0)
 
     def transform(c, halves):
         def one(step, carry):
@@ -141,15 +150,16 @@
                 sent[c, half, pl.ds(block * 16, 16)] = (
                     result[:, 128 * i : 128 * (i + 1)].astype(BF16).reshape(16, 16, 128)
                 )
-            for half in halves:
-                send_group(c, half, block)
             return carry
 
         lax.fori_loop(0, 4, one, 0)
         for half in halves:
-            got[c, half, s] = sent[c, half, s]
+            if (c, half) != (1, 0):
+                got[c, half, s] = sent[c, half, s]
 
     filter_half(1)
+    loads[2].wait()
+    transform(0, (1,))
     pl.semaphore_wait(barrier, GROUPS - 1 + BLOCKS - 1)
 
     edge = pltpu.make_async_remote_copy(
@@ -165,8 +175,7 @@
     def _():
         edge.start()
 
-    load_tables[0].wait()
-    transform(0, (1,))
+    send_all(0, 1)
 
     @pl.when(b == 0)
     def _():
@@ -178,30 +187,38 @@
 
     filter_half(0)
     transform(0, (0,))
-    load_tables[1].wait()
+    send_all(0, 0)
+    loads[3].wait()
     transform(1, (1, 0))
+    loads[4].wait()
 
     row = lax.broadcasted_iota(jnp.int32, (256, 256), 0)
     column = lax.broadcasted_iota(jnp.int32, (256, 256), 1)
     matches = (row // 16 == column % 16) & (row % 16 == column // 16)
     swap[...] = jnp.where(matches, 1.0, 0.0).astype(BF16)
-    for i in range(4):
-        place = lax.broadcasted_iota(jnp.int32, (128, STATIONS), 0) + 128 * i
-        station = (place % GROUPS) * LOCAL + place // GROUPS
-        hot = jnp.where(station == order_ref[...], 1.0, 0.0)
-        for j in range(4):
-            chosen[128 * j : 128 * (j + 1), 128 * i : 128 * (i + 1)] = (
-                hot[:, 128 * j : 128 * (j + 1)].T.astype(BF16)
-            )
-
-    def turn(c, half):
+
+    def prepare_chosen():
+        for i in range(4):
+            place = lax.broadcasted_iota(jnp.int32, (128, STATIONS), 0) + 128 * i
+            station = (place % GROUPS) * LOCAL + place // GROUPS
+            hot = jnp.where(station == order_ref[...], 1.0, 0.0)
+            for j in range(4):
+                chosen[128 * j : 128 * (j + 1), 128 * i : 128 * (i + 1)] = (
+                    hot[:, 128 * j : 128 * (j + 1)].T.astype(BF16)
+                )
+
+    def swapped(rows):
+        return dot(swap[...], rows.reshape(256, 128)).astype(BF16).reshape(16, 16, 128)
+
+    def arrived(c, half):
         others = pl.ds(0, GROUPS - 1)
         pltpu.make_async_copy(
-            sent.at[c, half, others], got.at[c, half, others], z_recv.at[c, half]
+            got.at[c, half, others], got.at[c, half, others], z_recv.at[c, half]
         ).wait()
-        for i in range(4):
-            rows = got[c, half, 16 * i : 16 * (i + 1)].reshape(256, 128)
-            rows = dot(swap[...], rows).astype(BF16).reshape(16, 16, 128)
+
+    def spread(c, half, source):
+        for i in range(4):
+            rows = swapped(source[c, half, 16 * i : 16 * (i + 1)])
             for x in range(16):
                 turned[c, half, x % 8, x // 8, 16 * i : 16 * (i + 1), :] = rows[x]
 
@@ -220,7 +237,7 @@
         lax.fori_loop(1, BLOCKS, one, 0)
         blocks[c, half, b] = turned[c, half, b]
 
-    def line_up(c, half):
+    def line_up(c, half, ahead=False):
         others = pl.ds(0, BLOCKS - 1)
         pltpu.make_async_copy(
             turned.at[c, half, others], blocks.at[c, half, others], x_recv.at[c, half]
@@ -244,71 +261,99 @@
                             )
                 for i in range(8):
                     place = pl.multiple_of(i * GROUPS + first, 16)
-                    column = 256 * p + 128 * half
-                    lanes[pl.ds(place, 16), column : column + 128] = held[i].astype(BF16)
+                    column = 256 * half + 128 * p
+                    if ahead:
+                        mixed[8 * p + i, pl.ds(first, 16), :] = held[i].astype(BF16)
+                    else:
+                        lanes[pl.ds(place, 16), column : column + 128] = held[i].astype(BF16)
             return carry
 
         lax.fori_loop(0, GROUPS // 16, one, 0)
 
+    def prepare_last():
+        line_up(1, 0, ahead=True)
+        for i in range(4):
+            rows = swapped(mixed[:, 16 * i : 16 * (i + 1), :])
+            sent[1, 0, 16 * i : 16 * (i + 1)] = rows
+        got[1, 0, s] = sent[1, 0, s]
+
+    def take_last():
+        for i in range(4):
+            rows = swapped(got[1, 0, 16 * i : 16 * (i + 1)])
+            for x in range(16):
+                place = x % 8 * GROUPS + 16 * i
+                column = 128 * (x // 8)
+                lanes[place : place + 16, column : column + 128] = rows[x]
+
+    def choose(half):
+        first = 256 * half
+        value = dot(chosen[...], lanes[:, first : first + 256])
+        pair[0, :, first : first + 256] = value.astype(BF16)
+        pair[1, :, first : first + 128] = value[:, 128:256].astype(BF16)
+        pair[1, :, first + 128 : first + 256] = (-value[:, 0:128]).astype(BF16)
+        for i in range(4):
+            total = jnp.zeros((1, 128), F32)
+            for j in range(2):
+                block = value[128 * i : 128 * (i + 1), 128 * j : 128 * (j + 1)].T
+                place = first + 128 * j
+                ordered_t[place : place + 128, 128 * i : 128 * (i + 1)] = block.astype(BF16)
+                total = total + jnp.sum(block * block, axis=0, keepdims=True)
+            power[half : half + 1, 128 * i : 128 * (i + 1)] = total
+
     def correlate(c):
-        def choose(i, carry):
-            rows = pl.ds(pl.multiple_of(i * 128, 128), 128)
-            value = dot(chosen[rows, :], lanes[...])
-            ordered[rows, :] = value.astype(BF16)
-            crossed[rows, 0:256] = value[:, 256:512].astype(BF16)
-            crossed[rows, 256:512] = (-value[:, 0:256]).astype(BF16)
-            for j in range(4):
-                ordered_t[128 * j : 128 * (j + 1), rows] = (
-                    value[:, 128 * j : 128 * (j + 1)].T.astype(BF16)
-                )
-            return carry
-
-        lax.fori_loop(0, 4, choose, 0)
-
-        def multiply(i, carry):
-            rows = pl.ds(pl.multiple_of(i * 128, 128), 128)
-            vis[0, rows, :] = dot(ordered[rows, :], ordered_t[...])
-            vis[1, rows, :] = dot(crossed[rows, :], ordered_t[...])
-            return carry
-
-        lax.fori_loop(0, 4, multiply, 0)
-        same = lax.broadcasted_iota(jnp.int32, (128, 128), 0) == lax.broadcasted_iota(
-            jnp.int32, (128, 128), 1
-        )
-        for i in range(4):
-            rows = slice(128 * i, 128 * (i + 1))
-            power = jnp.where(same, vis[0, rows, rows], 0.0)
-            col_scale[rows, :] = lax.rsqrt(jnp.sum(power, axis=1, keepdims=True) + epsilon)
-            row_scale[:, rows] = lax.rsqrt(jnp.sum(power, axis=0, keepdims=True) + epsilon)
+        scale = lax.rsqrt(power[0:1, :] + power[1:2, :] + epsilon)
+        row_scale[...] = scale
+        for i in range(4):
+            columns = slice(128 * i, 128 * (i + 1))
+            col_scale[columns, :] = jnp.broadcast_to(scale[:, columns], (128, 128)).T
 
         def finish(step, carry):
-            target = lax.rem(b + step, BLOCKS)
-            rows = pl.ds(pl.multiple_of(target * 64, 64), 64)
-            scale = col_scale[rows, :] * row_scale[...]
+            block = lax.rem(b // 2 + 1 + step, 4)
+            rows = pl.ds(pl.multiple_of(block * 128, 128), 128)
+            vis = dot(pair[:, rows, :].reshape(256, STATIONS), ordered_t[...])
             for q in range(2):
-                done[c, target, q] = (vis[q, rows, :] * scale).astype(BF16)
-
-            @pl.when(step < BLOCKS)
-            def _():
-                pltpu.make_async_remote_copy(
-                    src_ref=done.at[c, target],
-                    dst_ref=out_ref.at[:, 2 * b + c],
-                    send_sem=o_send.at[c],
-                    recv_sem=o_recv.at[c],
-                    device_id=(s, target),
-                    device_id_type=MESH,
-                ).start()
-
-            return carry
-
-        lax.fori_loop(1, BLOCKS + 1, finish, 0)
+                for j in range(4):
+                    columns = slice(128 * j, 128 * (j + 1))
+                    value = (
+                        vis[128 * q : 128 * (q + 1), columns]
+                        * col_scale[rows, :]
+                        * row_scale[:, columns]
+                    ).astype(BF16)
+                    for i in range(2):
+                        done[c, 2 * block + i, q, :, columns] = value[64 * i : 64 * (i + 1)]
+            for i in range(2):
+                target = 2 * block + i
+
+                @pl.when(target != b)
+                def _():
+                    pltpu.make_async_remote_copy(
+                        src_ref=done.at[c, target],
+                        dst_ref=out_ref.at[:, 2 * b + c],
+                        send_sem=o_send.at[c],
+                        recv_sem=o_recv.at[c],
+                        device_id=(s, target),
+                        device_id_type=MESH,
+                    ).start()
+
+            return carry
+
+        lax.fori_loop(0, 4, finish, 0)
         pltpu.make_async_copy(done.at[c, b], out_ref.at[:, 2 * b + c], own_sem.at[c]).start()
 
+    spread(1, 0, sent)
+    prepare_chosen()
+    prepare_last()
     for c in range(2):
-        turn(c, 1)
-        turn(c, 0)
-        line_up(c, 1)
-        line_up(c, 0)
+        for half in (1, 0):
+            arrived(c, half)
+            if (c, half) == (1, 0):
+                take_last()
+            else:
+                spread(c, half, got)
+                if c == 0:
+                    send_all(1, half)
+                line_up(c, half)
+            choose(half)
         correlate(c)
 
     @pl.when(b < BLOCKS - 1)
@@ -338,16 +383,17 @@
 
 def per_device(samples, fir_taps, station_order):
     anywhere = pl.BlockSpec(memory_space=pl.ANY)
-    near = pl.BlockSpec(memory_space=pltpu.VMEM)
     table = jnp.asarray(transform_table())
     dma = pltpu.SemaphoreType.DMA
     return pl.pallas_call(
         kernel,
         out_shape=jax.ShapeDtypeStruct((2, 16, 64, STATIONS), BF16),
-        in_specs=[anywhere, near, near, anywhere],
+        in_specs=[anywhere] * 4,
         out_specs=anywhere,
         scratch_shapes=[
             pltpu.VMEM(samples.shape, jnp.int32),
+            pltpu.VMEM(fir_taps.shape, F32),
+            pltpu.VMEM((1, STATIONS), jnp.int32),
             pltpu.VMEM(table.shape, BF16),
             pltpu.VMEM((TAPS - 1, 2 * LOCAL, CHANNELS), BF16),
             pltpu.VMEM((TAPS - 1, 2 * LOCAL, CHANNELS), BF16),
@@ -360,14 +406,14 @@
             pltpu.VMEM((STATIONS, STATIONS), BF16),
             pltpu.VMEM((256, 256), BF16),
             pltpu.VMEM((STATIONS, STATIONS), BF16),
+            pltpu.VMEM((2, STATIONS, STATIONS), BF16),
             pltpu.VMEM((STATIONS, STATIONS), BF16),
-            pltpu.VMEM((STATIONS, STATIONS), BF16),
-            pltpu.VMEM((STATIONS, STATIONS), BF16),
-            pltpu.VMEM((2, STATIONS, STATIONS), F32),
-            pltpu.VMEM((STATIONS, 1), F32),
+            pltpu.VMEM((2, STATIONS), F32),
+            pltpu.VMEM((STATIONS, 128), F32),
             pltpu.VMEM((1, STATIONS), F32),
             pltpu.VMEM((2, BLOCKS, 2, 64, STATIONS), BF16),
-            dma((3,)),
+            pltpu.VMEM((16, GROUPS, 128), BF16),
+            dma((5,)),
             dma((2,)),
             dma((2, 2)),
             dma((2, 2)),
@@ -378,7 +424,7 @@
             dma((2,)),
         ],
         compiler_params=pltpu.CompilerParams(
-            collective_id=0, has_side_effects=True, vmem_limit_bytes=48 << 20
+            collective_id=0, has_side_effects=True, vmem_limit_bytes=61900 << 10
         ),
         cost_estimate=pl.CostEstimate(
             flops=4_000_000_000, bytes_accessed=14_000_000, transcendentals=2048

time: 99 us -> 91.1 us (0.920)
  Pallas kernels: 94.4 us -> 87.8 us
  local copies, waits for them, and re-layouts: 4.35 us -> 3.13 us
    pallas_call x1, Pallas kernels: 94.4 us -> 87.8 us  [per_device(): pl.pallas_call(kernel, out_shape=jax.ShapeDtypeStruct((2, 16, 64, STATION...]
    unnamed x7 -> x1, local copies, waits for them, and re-layouts: 4.35 us -> 3.13 us
where the time goes in v3:
time: 91.1 us; the launch traced here: 90.9 us
  Pallas kernels  87.8 us (96%)
  local copies, waits for them, and re-layouts  3.13 us (3%)
    pallas_call x1, Pallas kernels, per_device(): pl.pallas_call(kernel, out_shape=jax.ShapeDtypeStruct((2, 16, 64, STATION...  87.8 us
    unnamed x1, local copies, waits for them, and re-layouts  3.13 us

profile of v3, /device:TPU:1, one launch (start us, length us, event | category | flops | bytes accessed | tf_op | source)
XLA Modules:
  0.0 90.9 jit_solution(7361363292769615612)
XLA Ops:
  0.0 87.8 %shard_map.46 = bf16[2,16,64,512]{3,2,1,0:T(8,128)(2,1)} custom-call(s32[2,8,32768]{2,1,0:T(8,128)} %samples_ref.1, f32[8,1024]{1,0:T(8,128)} %taps_in.1, s32[1,512]{1,0:T(1,128)} %bitcast.1, bf16[2,1024,2048]{2,1,0:T(8,128)(2,1)} %constant.2.clone.table_ref), custom_call_target="tpu_custom_call" | custom-call | flops 4000000000 | bytes 14000000 | tf_op jit(solution)/shard_map/pallas_call | solution.py:388
  87.8 3.1 %copy.6 = bf16[2,16,64,512]{3,2,1,0:T(8,128)(2,1)} copy(bf16[2,16,64,512]{3,2,1,0:T(8,128)(2,1)} %shard_map.46) | data formatting | bytes 4194304

commit v4 on v3

--- a/solution.py
+++ b/solution.py
@@ -138,6 +138,30 @@
 
         lax.fori_loop(1, GROUPS // 2, one, 0)
 
+    def send_last():
+        def early(step, carry):
+            place = lax.rem(s + step, 16)
+            target = place // 8 * 32 + lax.rem(place, 8)
+
+            @pl.when(target != s)
+            def _():
+                send(1, 0, target)
+
+            return carry
+
+        def late(step, carry):
+            offset = GROUPS // 2 - (step + 1) // 2
+            target = lax.rem(s + GROUPS + offset * (1 - 2 * lax.rem(step, 2)), GROUPS)
+
+            @pl.when(lax.rem(target, 32) >= 8)
+            def _():
+                send(1, 0, target)
+
+            return carry
+
+        lax.fori_loop(0, 16, early, 0)
+        lax.fori_loop(0, GROUPS - 1, late, 0)
+
     def transform(c, halves):
         def one(step, carry):
             block = lax.rem(s // 16 + step, 4)
@@ -350,8 +374,10 @@
                 take_last()
             else:
                 spread(c, half, got)
-                if c == 0:
+                if c == 0 and half == 1:
                     send_all(1, half)
+                elif c == 0:
+                    send_last()
                 line_up(c, half)
             choose(half)
         correlate(c)

time: 91.1 us -> 91.1 us (level)
  no operation moved by 1% of the time
where the time goes in v4:
time: 91.1 us; the launch traced here: 90.9 us
  Pallas kernels  87.8 us (96%)
  local copies, waits for them, and re-layouts  3.13 us (3%)
    pallas_call x1, Pallas kernels, per_device(): pl.pallas_call(kernel, out_shape=jax.ShapeDtypeStruct((2, 16, 64, STATION...  87.8 us
    unnamed x1, local copies, waits for them, and re-layouts  3.13 us

profile of v4, /device:TPU:1, one launch (start us, length us, event | category | flops | bytes accessed | tf_op | source)
XLA Modules:
  0.0 90.9 jit_solution(17602403394184184659)
XLA Ops:
  0.0 87.8 %shard_map.46 = bf16[2,16,64,512]{3,2,1,0:T(8,128)(2,1)} custom-call(s32[2,8,32768]{2,1,0:T(8,128)} %samples_ref.1, f32[8,1024]{1,0:T(8,128)} %taps_in.1, s32[1,512]{1,0:T(1,128)} %bitcast.1, bf16[2,1024,2048]{2,1,0:T(8,128)(2,1)} %constant.2.clone.table_ref), custom_call_target="tpu_custom_call" | custom-call | flops 4000000000 | bytes 14000000 | tf_op jit(solution)/shard_map/pallas_call | solution.py:414
  87.8 3.1 %copy.6 = bf16[2,16,64,512]{3,2,1,0:T(8,128)(2,1)} copy(bf16[2,16,64,512]{3,2,1,0:T(8,128)(2,1)} %shard_map.46) | data formatting | bytes 4194304
